TPU v7x, 32 devices: a whole 2x2x4 slice. The times are simulated.
32 devices in a mesh: shift: 4 (over y, core), space: 8 (over z, x).
Axes of the slice: x: 2, y: 2, z: 4, core: 2. Of those that a mesh axis runs over, the one named last changes fastest.
Arguments:
- coefficients: float32 [4, 2, 2, 8, 32, 512], P('shift', None, None, 'space'), may hold values from -0.18 to 0.18
- source: float32 [8, 8, 8, 256], P('space'), may hold values from -26 to 26
Outputs:
- pressure_mean: float32 [8, 8, 8, 256], P('space')
- pressure_variance: float32 [8, 8, 8, 256], P('space')
All inputs are finite; a program needn't handle non-finite values.
Results may differ from a plain program's by a relative error of at most 0.0004.
Values sent between devices are 32-bit elements; how exact they have to be, the bound alone decides.
A program may use at most 64 MiB of HBM per device.

v0:
```python
import math

import jax
import jax.numpy as jnp
from jax import lax
from jax.sharding import PartitionSpec as P

ITERS = 4


reaction = 0.02
low_bound = 0.05
high_bound = 2.0
centre = 0.5 * (low_bound + high_bound)
half_width = 0.5 * (high_bound - low_bound)
sigma_one = centre / half_width


def passed_along(value, axis, steps):
    count = lax.axis_size(axis)
    first, last = (max(0, -steps), min(count, count - steps))
    return lax.ppermute(value, axis, [(source, source + steps) for source in range(first, last)])


def harmonic(left, right):
    return 2.0 * left * right / (left + right)


def carry_first(layer, offset):
    return passed_along(layer, "space", offset)


def carry_second(layer, offset):
    return passed_along(layer, "space", offset)


def lower_and_upper(
    pressure_field, which_axis, index_step, axis_position, bricks_along, halo_holder
):
    extent = pressure_field.shape[which_axis]
    highest_layer = lax.slice_in_dim(pressure_field, extent - 1, extent, axis=which_axis)
    lowest_layer = lax.slice_in_dim(pressure_field, 0, 1, axis=which_axis)
    lower_mask = (axis_position > 0).astype(jnp.float32)
    upper_mask = (axis_position < bricks_along - 1).astype(jnp.float32)
    received_below = halo_holder(highest_layer, index_step) * lower_mask
    received_above = halo_holder(lowest_layer, -index_step) * upper_mask
    lower = jnp.concatenate(
        [received_below, lax.slice_in_dim(pressure_field, 0, extent - 1, axis=which_axis)],
        axis=which_axis,
    )
    upper = jnp.concatenate(
        [lax.slice_in_dim(pressure_field, 1, extent, axis=which_axis), received_above],
        axis=which_axis,
    )
    return (lower, upper)


def along_depth(pressure_field, which_axis):
    extent = pressure_field.shape[which_axis]
    blank = jnp.zeros_like(lax.slice_in_dim(pressure_field, 0, 1, axis=which_axis))
    lower = jnp.concatenate(
        [blank, lax.slice_in_dim(pressure_field, 0, extent - 1, axis=which_axis)], axis=which_axis
    )
    upper = jnp.concatenate(
        [lax.slice_in_dim(pressure_field, 1, extent, axis=which_axis), blank], axis=which_axis
    )
    return (lower, upper)


def operate(pressure_field, weight_list, finders):
    total = reaction * pressure_field
    for which_axis in range(3):
        lower, upper = finders[which_axis](pressure_field)
        weight_lower, weight_upper = weight_list[which_axis]
        total = (
            total
            + weight_upper * (pressure_field - upper)
            + weight_lower * (pressure_field - lower)
        )
    return total


def shards(coefficients, source):
    n_space = lax.axis_size("space")
    bricks_first = max(2, n_space // 8)
    bricks_second = n_space // bricks_first
    position = lax.axis_index("space")
    brick_x = position // bricks_second
    brick_y = position % bricks_second
    local = coefficients[0]
    modes_count = local.shape[-1]
    columns = local.shape[3]
    cells_z = modes_count // 2
    pencils = local.reshape(2, bricks_first * columns, modes_count)
    modes = lax.broadcasted_iota(jnp.int32, (modes_count, cells_z), 0)
    cells = lax.broadcasted_iota(jnp.int32, (modes_count, cells_z), 1)
    angle = (modes * cells % modes_count).astype(jnp.float32) * (2.0 * math.pi / modes_count)
    logperm = jnp.dot(
        pencils[0],
        jnp.cos(angle),
        precision=lax.Precision.HIGHEST,
        preferred_element_type=jnp.float32,
    )
    logperm = logperm + jnp.dot(
        pencils[1],
        jnp.sin(angle),
        precision=lax.Precision.HIGHEST,
        preferred_element_type=jnp.float32,
    )
    perm_rows = jnp.exp(logperm)
    brick_cols = columns // bricks_second
    n_shift = lax.axis_size("shift")
    outgoing = perm_rows.reshape(n_space, 1, brick_cols, cells_z)
    arrived = lax.all_to_all(outgoing, "space", split_axis=0, concat_axis=1, tiled=True)
    perm = arrived.reshape(n_space, brick_cols, cells_z)

    def find_first(pressure_field):
        return lower_and_upper(pressure_field, 0, bricks_second, brick_x, bricks_first, carry_first)

    def find_second(pressure_field):
        return lower_and_upper(pressure_field, 1, 1, brick_y, bricks_second, carry_second)

    def find_third(pressure_field):
        return along_depth(pressure_field, 2)

    residual = source[0]
    finders = [find_first, find_second, find_third]
    weight_list = []
    diagonal = reaction + jnp.zeros_like(perm)
    for which_axis in range(3):
        lower, upper = finders[which_axis](perm)
        weight_lower = harmonic(perm, lower)
        weight_upper = harmonic(perm, upper)
        weight_list.append((weight_lower, weight_upper))
        diagonal = diagonal + (weight_lower + weight_upper)
    pressure = jnp.zeros_like(perm)
    direction = residual / diagonal / centre
    ratio_now = 1.0 / sigma_one
    for sweep_index in range(ITERS):
        pressure = pressure + direction
        residual = residual - operate(direction, weight_list, finders)
        ratio_next = 1.0 / (2.0 * sigma_one - ratio_now)
        direction = ratio_next * ratio_now * direction + 2.0 * ratio_next / half_width * (
            residual / diagonal
        )
        ratio_now = ratio_next
    pressure = pressure + direction
    first, second = lax.psum((pressure, pressure * pressure), "shift")
    pressure_mean = first / n_shift
    pressure_variance = (second - first * pressure_mean) / (n_shift - 1)
    return (pressure_mean[None], pressure_variance[None])


def solution(mesh):
    in_specs = (P("shift", None, None, "space", None, None), P("space", None, None, None))
    out_specs = (P("space", None, None, None), P("space", None, None, None))
    return jax.shard_map(shards, mesh=mesh, in_specs=in_specs, out_specs=out_specs, check_vma=False)
```

profile of v0, /device:TPU:0, one launch (start us, length us, event | category | flops | bytes accessed | tf_op | source)
XLA Modules:
  0.0 145.1 jit_solution(5426519292635868424)
XLA Ops:
  7.2 1.0 fusion.73
  8.2 2.4 %fusion.6 = f32[256,64]{0,1:T(8,128)S(1)} fusion(f32[64,512]{1,0:T(8,128)S(1)} %bitcast.85), kind=kOutput, calls=%fused_computation.10 | convolution fusion | flops 102498304 | bytes 196608 | tf_op jit(solution)/shard_map/dot_general | solution.py:98
  10.5 3.0 %fusion.1 = f32[8,1,8,256]{3,2,1,0:T(8,128)} fusion(f32[256,64]{0,1:T(8,128)S(1)} %fusion.6, f32[64,512]{1,0:T(8,128)S(1)} %bitcast.84), kind=kOutput, calls=%fused_computation.2 | convolution fusion | flops 102514688 | bytes 262144 | tf_op jit(solution)/shard_map/dot_general | solution.py:104
  13.5 7.3 %all-to-all-start = ((f32[8,1,8,256]{3,2,1,0:T(8,128)}), f32[8,1,8,256]{3,2,1,0:T(8,128)S(1)}, u32[]{:S(2)}, u32[]{:S(2)}) async-start(f32[8,1,8,256]{3,2,1,0:T(8,128)} %fusion.1), calls=%async_computation | async-start | bytes 131072 | tf_op jit(solution)/shard_map/all_to_all | solution.py:114
  20.9 6.8 %all-to-all-done = f32[8,1,8,256]{3,2,1,0:T(8,128)S(1)} async-done(((f32[8,1,8,256]{3,2,1,0:T(8,128)}), f32[8,1,8,256]{3,2,1,0:T(8,128)S(1)}, u32[]{:S(2)}, u32[]{:S(2)}) %all-to-all-start) | async-done | bytes 65568 | tf_op jit(solution)/shard_map/all_to_all | solution.py:114
  27.8 2.4 %collective-permute-start = (f32[1,8,256]{2,1,0:T(8,128)S(1)}, f32[1,8,256]{2,1,0:T(8,128)S(1)}, u32[]{:S(2)}, u32[]{:S(2)}) collective-permute-start(f32[1,8,256]{2,1,0:T(8,128)S(1)} %get-tuple-element.68), channel_id=1, source_target_pairs={{0,4},{1,5},{2,6},{3,7},{8,12},{9,13},{10,14},{11,15},{16,20},{17,... | collective-permute-start | bytes 24584 | tf_op jit(solution)/shard_map/ppermute | solution.py:22
  30.2 1.3 collective-permute-start.1
  31.5 2.3 %collective-permute-start.2 = (f32[8,1,256]{2,1,0:T(1,128)S(1)}, f32[8,1,256]{2,1,0:T(1,128)S(1)}, u32[]{:S(2)}, u32[]{:S(2)}) collective-permute-start(f32[8,1,256]{2,1,0:T(1,128)S(1)} %get-tuple-element.64), channel_id=1, source_target_pairs={{0,1},{1,2},{2,3},{3,4},{4,5},{5,6},{6,7},{8,9},{9,10},{10,11},{11... | collective-permute-start | bytes 24584 | tf_op jit(solution)/shard_map/ppermute | solution.py:22
  33.8 1.3 collective-permute-start.3
  35.2 4.2 %collective-permute-done.3 = f32[8,1,256]{2,1,0:T(1,128)S(1)} collective-permute-done((f32[8,1,256]{2,1,0:T(1,128)S(1)}, f32[8,1,256]{2,1,0:T(1,128)S(1)}, u32[]{:S(2)}, u32[]{:S(2)}) %collective-permute-start.3) | collective-permute-done | bytes 8224 | tf_op jit(solution)/shard_map/ppermute | solution.py:22
  39.7 1.3 collective-permute-start.6
  41.0 1.3 collective-permute-start.4
  42.3 9.5 %collective-permute-start.5 = (f32[1,8,256]{2,1,0:T(8,128)S(1)}, f32[1,8,256]{2,1,0:T(8,128)S(1)}, u32[]{:S(2)}, u32[]{:S(2)}) collective-permute-start(f32[1,8,256]{2,1,0:T(8,128)S(1)} %get-tuple-element.55), channel_id=1, source_target_pairs={{0,4},{1,5},{2,6},{3,7},{8,12},{9,13},{10,14},{11,15},{16,20},{17,... | collective-permute-start | bytes 24584 | tf_op jit(solution)/shard_map/ppermute | solution.py:22
  51.8 1.3 collective-permute-start.7
  53.1 1.3 collective-permute-done.7
  54.7 1.3 collective-permute-start.10
  56.0 5.3 %collective-permute-start.11 = (f32[8,1,256]{2,1,0:T(1,128)S(1)}, f32[8,1,256]{2,1,0:T(1,128)S(1)}, u32[]{:S(2)}, u32[]{:S(2)}) collective-permute-start(f32[8,1,256]{2,1,0:T(1,128)S(1)} %get-tuple-element.49), channel_id=1, source_target_pairs={{0,1},{1,2},{2,3},{3,4},{4,5},{5,6},{6,7},{8,9},{9,10},{10,11},{11... | collective-permute-start | bytes 24584 | tf_op jit(solution)/shard_map/ppermute | solution.py:22
  61.3 1.3 collective-permute-start.8
  62.6 5.6 %collective-permute-start.9 = (f32[1,8,256]{2,1,0:T(8,128)S(1)}, f32[1,8,256]{2,1,0:T(8,128)S(1)}, u32[]{:S(2)}, u32[]{:S(2)}) collective-permute-start(f32[1,8,256]{2,1,0:T(8,128)S(1)} %get-tuple-element.45), channel_id=1, source_target_pairs={{0,4},{1,5},{2,6},{3,7},{8,12},{9,13},{10,14},{11,15},{16,20},{17,... | collective-permute-start | bytes 24584 | tf_op jit(solution)/shard_map/ppermute | solution.py:22
  68.3 1.3 collective-permute-done.9
  69.8 1.3 collective-permute-start.14
  71.2 5.5 %collective-permute-start.15 = (f32[8,1,256]{2,1,0:T(1,128)S(1)}, f32[8,1,256]{2,1,0:T(1,128)S(1)}, u32[]{:S(2)}, u32[]{:S(2)}) collective-permute-start(f32[8,1,256]{2,1,0:T(1,128)S(1)} %get-tuple-element.39), channel_id=1, source_target_pairs={{0,1},{1,2},{2,3},{3,4},{4,5},{5,6},{6,7},{8,9},{9,10},{10,11},{11... | collective-permute-start | bytes 24584 | tf_op jit(solution)/shard_map/ppermute | solution.py:22
  76.7 1.3 collective-permute-start.12
  78.0 5.4 %collective-permute-start.13 = (f32[1,8,256]{2,1,0:T(8,128)S(1)}, f32[1,8,256]{2,1,0:T(8,128)S(1)}, u32[]{:S(2)}, u32[]{:S(2)}) collective-permute-start(f32[1,8,256]{2,1,0:T(8,128)S(1)} %get-tuple-element.35), channel_id=1, source_target_pairs={{0,4},{1,5},{2,6},{3,7},{8,12},{9,13},{10,14},{11,15},{16,20},{17,... | collective-permute-start | bytes 24584 | tf_op jit(solution)/shard_map/ppermute | solution.py:22
  83.5 1.3 collective-permute-done.13
  85.1 1.3 collective-permute-start.18
  86.4 5.4 %collective-permute-start.19 = (f32[8,1,256]{2,1,0:T(1,128)S(1)}, f32[8,1,256]{2,1,0:T(1,128)S(1)}, u32[]{:S(2)}, u32[]{:S(2)}) collective-permute-start(f32[8,1,256]{2,1,0:T(1,128)S(1)} %get-tuple-element.29), channel_id=1, source_target_pairs={{0,1},{1,2},{2,3},{3,4},{4,5},{5,6},{6,7},{8,9},{9,10},{10,11},{11... | collective-permute-start | bytes 24584 | tf_op jit(solution)/shard_map/ppermute | solution.py:22
  91.8 1.3 collective-permute-start.16
  93.1 5.4 %collective-permute-start.17 = (f32[1,8,256]{2,1,0:T(8,128)S(1)}, f32[1,8,256]{2,1,0:T(8,128)S(1)}, u32[]{:S(2)}, u32[]{:S(2)}) collective-permute-start(f32[1,8,256]{2,1,0:T(8,128)S(1)} %get-tuple-element.25), channel_id=1, source_target_pairs={{0,4},{1,5},{2,6},{3,7},{8,12},{9,13},{10,14},{11,15},{16,20},{17,... | collective-permute-start | bytes 24584 | tf_op jit(solution)/shard_map/ppermute | solution.py:22
  98.6 1.3 collective-permute-done.17
  100.8 35.9 %all-reduce.13.cloned.1.call-done = (f32[8,8,256]{2,1,0:T(8,128)}, f32[8,8,256]{2,1,0:T(8,128)}) async-done(((f32[8,8,256]{2,1,0:T(8,128)}, f32[8,8,256]{2,1,0:T(8,128)}), (f32[8,8,256]{2,1,0:T(8,128)}, f32[8,8,256]{2,1,0:T(8,128)})) %all-reduce.13.cloned.1.call-update) | async-done | bytes 131088 | tf_op jit(solution)/shard_map/psum | solution.py:148
  136.7 1.5 %fusion.15 = (f32[1,8,8,256]{3,2,1,0:T(8,128)}, f32[1,8,8,256]{3,2,1,0:T(8,128)}) fusion(f32[8,8,256]{2,1,0:T(8,128)} %get-tuple-element.3, f32[8,8,256]{2,1,0:T(8,128)} %get-tuple-element.2), kind=kLoop, calls=%fused_computation.19 | loop fusion | flops 65536 | bytes 262144 | tf_op jit(solution)/shard_map/broadcast_in_dim | solution.py:151
  (70 shorter events, 2.1 us)
Async XLA Ops:
  13.5 14.2 %all-to-all-start = ((f32[8,1,8,256]{3,2,1,0:T(8,128)}), f32[8,1,8,256]{3,2,1,0:T(8,128)S(1)}, u32[]{:S(2)}, u32[]{:S(2)}) async-start(f32[8,1,8,256]{3,2,1,0:T(8,128)} %fusion.1), calls=%async_computation | async-start | bytes 131072 | tf_op jit(solution)/shard_map/all_to_all | solution.py:114
  20.8 115.9 %all-reduce.13.cloned.1.call-start = ((), (), s32[]{:S(2)}) async-start(), calls=%async_computation.1 | async-start | bytes 262144 | tf_op jit(solution)/shard_map/psum | solution.py:148
  27.8 11.5 %collective-permute-start = (f32[1,8,256]{2,1,0:T(8,128)S(1)}, f32[1,8,256]{2,1,0:T(8,128)S(1)}, u32[]{:S(2)}, u32[]{:S(2)}) collective-permute-start(f32[1,8,256]{2,1,0:T(8,128)S(1)} %get-tuple-element.68), channel_id=1, source_target_pairs={{0,4},{1,5},{2,6},{3,7},{8,12},{9,13},{10,14},{11,15},{16,20},{17,... | collective-permute-start | bytes 24584 | tf_op jit(solution)/shard_map/ppermute | solution.py:22
  30.2 9.2 %collective-permute-start.1 = (f32[1,8,256]{2,1,0:T(8,128)S(1)}, f32[1,8,256]{2,1,0:T(8,128)S(1)}, u32[]{:S(2)}, u32[]{:S(2)}) collective-permute-start(f32[1,8,256]{2,1,0:T(8,128)S(1)} %get-tuple-element.69), channel_id=1, source_target_pairs={{4,0},{5,1},{6,2},{7,3},{12,8},{13,9},{14,10},{15,11},{20,16},{21,... | collective-permute-start | bytes 24584 | tf_op jit(solution)/shard_map/ppermute | solution.py:22
  31.5 3.6 %collective-permute-start.2 = (f32[8,1,256]{2,1,0:T(1,128)S(1)}, f32[8,1,256]{2,1,0:T(1,128)S(1)}, u32[]{:S(2)}, u32[]{:S(2)}) collective-permute-start(f32[8,1,256]{2,1,0:T(1,128)S(1)} %get-tuple-element.64), channel_id=1, source_target_pairs={{0,1},{1,2},{2,3},{3,4},{4,5},{5,6},{6,7},{8,9},{9,10},{10,11},{11... | collective-permute-start | bytes 24584 | tf_op jit(solution)/shard_map/ppermute | solution.py:22
  33.8 5.5 %collective-permute-start.3 = (f32[8,1,256]{2,1,0:T(1,128)S(1)}, f32[8,1,256]{2,1,0:T(1,128)S(1)}, u32[]{:S(2)}, u32[]{:S(2)}) collective-permute-start(f32[8,1,256]{2,1,0:T(1,128)S(1)} %get-tuple-element.65), channel_id=1, source_target_pairs={{1,0},{2,1},{3,2},{4,3},{5,4},{6,5},{7,6},{9,8},{10,9},{11,10},{12... | collective-permute-start | bytes 24584 | tf_op jit(solution)/shard_map/ppermute | solution.py:22
  35.1 4.3 %copy-start = (f32[1,8,8,256]{3,2,1,0:T(8,128)S(1)}, f32[1,8,8,256]{3,2,1,0:T(8,128)}, u32[]{:S(2)}) copy-start(f32[1,8,8,256]{3,2,1,0:T(8,128)} %param.3) | copy-start | bytes 196612
  39.7 13.4 %collective-permute-start.6 = (f32[8,1,256]{2,1,0:T(1,128)S(1)}, f32[8,1,256]{2,1,0:T(1,128)S(1)}, u32[]{:S(2)}, u32[]{:S(2)}) collective-permute-start(f32[8,1,256]{2,1,0:T(1,128)S(1)} %get-tuple-element.58), channel_id=1, source_target_pairs={{1,0},{2,1},{3,2},{4,3},{5,4},{6,5},{7,6},{9,8},{10,9},{11,10},{12... | collective-permute-start | bytes 24584 | tf_op jit(solution)/shard_map/ppermute | solution.py:22
  41.0 13.5 %collective-permute-start.4 = (f32[1,8,256]{2,1,0:T(8,128)S(1)}, f32[1,8,256]{2,1,0:T(8,128)S(1)}, u32[]{:S(2)}, u32[]{:S(2)}) collective-permute-start(f32[1,8,256]{2,1,0:T(8,128)S(1)} %get-tuple-element.54), channel_id=1, source_target_pairs={{4,0},{5,1},{6,2},{7,3},{12,8},{13,9},{14,10},{15,11},{20,16},{21,... | collective-permute-start | bytes 24584 | tf_op jit(solution)/shard_map/ppermute | solution.py:22
  42.3 12.2 %collective-permute-start.5 = (f32[1,8,256]{2,1,0:T(8,128)S(1)}, f32[1,8,256]{2,1,0:T(8,128)S(1)}, u32[]{:S(2)}, u32[]{:S(2)}) collective-permute-start(f32[1,8,256]{2,1,0:T(8,128)S(1)} %get-tuple-element.55), channel_id=1, source_target_pairs={{0,4},{1,5},{2,6},{3,7},{8,12},{9,13},{10,14},{11,15},{16,20},{17,... | collective-permute-start | bytes 24584 | tf_op jit(solution)/shard_map/ppermute | solution.py:22
  51.8 2.6 %collective-permute-start.7 = (f32[8,1,256]{2,1,0:T(1,128)S(1)}, f32[8,1,256]{2,1,0:T(1,128)S(1)}, u32[]{:S(2)}, u32[]{:S(2)}) collective-permute-start(f32[8,1,256]{2,1,0:T(1,128)S(1)} %get-tuple-element.59), channel_id=1, source_target_pairs={{0,1},{1,2},{2,3},{3,4},{4,5},{5,6},{6,7},{8,9},{9,10},{10,11},{11... | collective-permute-start | bytes 24584 | tf_op jit(solution)/shard_map/ppermute | solution.py:22
  54.7 13.5 %collective-permute-start.10 = (f32[8,1,256]{2,1,0:T(1,128)S(1)}, f32[8,1,256]{2,1,0:T(1,128)S(1)}, u32[]{:S(2)}, u32[]{:S(2)}) collective-permute-start(f32[8,1,256]{2,1,0:T(1,128)S(1)} %get-tuple-element.48), channel_id=1, source_target_pairs={{1,0},{2,1},{3,2},{4,3},{5,4},{6,5},{7,6},{9,8},{10,9},{11,10},{12... | collective-permute-start | bytes 24584 | tf_op jit(solution)/shard_map/ppermute | solution.py:22
  56.0 12.2 %collective-permute-start.11 = (f32[8,1,256]{2,1,0:T(1,128)S(1)}, f32[8,1,256]{2,1,0:T(1,128)S(1)}, u32[]{:S(2)}, u32[]{:S(2)}) collective-permute-start(f32[8,1,256]{2,1,0:T(1,128)S(1)} %get-tuple-element.49), channel_id=1, source_target_pairs={{0,1},{1,2},{2,3},{3,4},{4,5},{5,6},{6,7},{8,9},{9,10},{10,11},{11... | collective-permute-start | bytes 24584 | tf_op jit(solution)/shard_map/ppermute | solution.py:22
  61.3 7.0 %collective-permute-start.8 = (f32[1,8,256]{2,1,0:T(8,128)S(1)}, f32[1,8,256]{2,1,0:T(8,128)S(1)}, u32[]{:S(2)}, u32[]{:S(2)}) collective-permute-start(f32[1,8,256]{2,1,0:T(8,128)S(1)} %get-tuple-element.44), channel_id=1, source_target_pairs={{4,0},{5,1},{6,2},{7,3},{12,8},{13,9},{14,10},{15,11},{20,16},{21,... | collective-permute-start | bytes 24584 | tf_op jit(solution)/shard_map/ppermute | solution.py:22
  62.6 7.0 %collective-permute-start.9 = (f32[1,8,256]{2,1,0:T(8,128)S(1)}, f32[1,8,256]{2,1,0:T(8,128)S(1)}, u32[]{:S(2)}, u32[]{:S(2)}) collective-permute-start(f32[1,8,256]{2,1,0:T(8,128)S(1)} %get-tuple-element.45), channel_id=1, source_target_pairs={{0,4},{1,5},{2,6},{3,7},{8,12},{9,13},{10,14},{11,15},{16,20},{17,... | collective-permute-start | bytes 24584 | tf_op jit(solution)/shard_map/ppermute | solution.py:22
  69.8 13.6 %collective-permute-start.14 = (f32[8,1,256]{2,1,0:T(1,128)S(1)}, f32[8,1,256]{2,1,0:T(1,128)S(1)}, u32[]{:S(2)}, u32[]{:S(2)}) collective-permute-start(f32[8,1,256]{2,1,0:T(1,128)S(1)} %get-tuple-element.38), channel_id=1, source_target_pairs={{1,0},{2,1},{3,2},{4,3},{5,4},{6,5},{7,6},{9,8},{10,9},{11,10},{12... | collective-permute-start | bytes 24584 | tf_op jit(solution)/shard_map/ppermute | solution.py:22
  71.2 12.3 %collective-permute-start.15 = (f32[8,1,256]{2,1,0:T(1,128)S(1)}, f32[8,1,256]{2,1,0:T(1,128)S(1)}, u32[]{:S(2)}, u32[]{:S(2)}) collective-permute-start(f32[8,1,256]{2,1,0:T(1,128)S(1)} %get-tuple-element.39), channel_id=1, source_target_pairs={{0,1},{1,2},{2,3},{3,4},{4,5},{5,6},{6,7},{8,9},{9,10},{10,11},{11... | collective-permute-start | bytes 24584 | tf_op jit(solution)/shard_map/ppermute | solution.py:22
  76.7 6.8 %collective-permute-start.12 = (f32[1,8,256]{2,1,0:T(8,128)S(1)}, f32[1,8,256]{2,1,0:T(8,128)S(1)}, u32[]{:S(2)}, u32[]{:S(2)}) collective-permute-start(f32[1,8,256]{2,1,0:T(8,128)S(1)} %get-tuple-element.34), channel_id=1, source_target_pairs={{4,0},{5,1},{6,2},{7,3},{12,8},{13,9},{14,10},{15,11},{20,16},{21,... | collective-permute-start | bytes 24584 | tf_op jit(solution)/shard_map/ppermute | solution.py:22
  78.0 6.8 %collective-permute-start.13 = (f32[1,8,256]{2,1,0:T(8,128)S(1)}, f32[1,8,256]{2,1,0:T(8,128)S(1)}, u32[]{:S(2)}, u32[]{:S(2)}) collective-permute-start(f32[1,8,256]{2,1,0:T(8,128)S(1)} %get-tuple-element.35), channel_id=1, source_target_pairs={{0,4},{1,5},{2,6},{3,7},{8,12},{9,13},{10,14},{11,15},{16,20},{17,... | collective-permute-start | bytes 24584 | tf_op jit(solution)/shard_map/ppermute | solution.py:22
  85.1 13.5 %collective-permute-start.18 = (f32[8,1,256]{2,1,0:T(1,128)S(1)}, f32[8,1,256]{2,1,0:T(1,128)S(1)}, u32[]{:S(2)}, u32[]{:S(2)}) collective-permute-start(f32[8,1,256]{2,1,0:T(1,128)S(1)} %get-tuple-element.28), channel_id=1, source_target_pairs={{1,0},{2,1},{3,2},{4,3},{5,4},{6,5},{7,6},{9,8},{10,9},{11,10},{12... | collective-permute-start | bytes 24584 | tf_op jit(solution)/shard_map/ppermute | solution.py:22
  86.4 12.2 %collective-permute-start.19 = (f32[8,1,256]{2,1,0:T(1,128)S(1)}, f32[8,1,256]{2,1,0:T(1,128)S(1)}, u32[]{:S(2)}, u32[]{:S(2)}) collective-permute-start(f32[8,1,256]{2,1,0:T(1,128)S(1)} %get-tuple-element.29), channel_id=1, source_target_pairs={{0,1},{1,2},{2,3},{3,4},{4,5},{5,6},{6,7},{8,9},{9,10},{10,11},{11... | collective-permute-start | bytes 24584 | tf_op jit(solution)/shard_map/ppermute | solution.py:22
  91.8 6.8 %collective-permute-start.16 = (f32[1,8,256]{2,1,0:T(8,128)S(1)}, f32[1,8,256]{2,1,0:T(8,128)S(1)}, u32[]{:S(2)}, u32[]{:S(2)}) collective-permute-start(f32[1,8,256]{2,1,0:T(8,128)S(1)} %get-tuple-element.24), channel_id=1, source_target_pairs={{4,0},{5,1},{6,2},{7,3},{12,8},{13,9},{14,10},{15,11},{20,16},{21,... | collective-permute-start | bytes 24584 | tf_op jit(solution)/shard_map/ppermute | solution.py:22
  93.1 6.8 %collective-permute-start.17 = (f32[1,8,256]{2,1,0:T(8,128)S(1)}, f32[1,8,256]{2,1,0:T(8,128)S(1)}, u32[]{:S(2)}, u32[]{:S(2)}) collective-permute-start(f32[1,8,256]{2,1,0:T(8,128)S(1)} %get-tuple-element.25), channel_id=1, source_target_pairs={{0,4},{1,5},{2,6},{3,7},{8,12},{9,13},{10,14},{11,15},{16,20},{17,... | collective-permute-start | bytes 24584 | tf_op jit(solution)/shard_map/ppermute | solution.py:22
Sparse Core Ops, SparseCore 0:
  100.9 35.7 all-reduce.12
where the time goes:
time: 146 us; the launch traced here: 145 us
  starting transfers between devices  68.4 us (47%)
  waiting for transfers between devices  52.1 us (36%)
  between operations  14.6 us (10%)
  matrix products  5.39 us (4%)
  other arithmetic  2.95 us (2%)
  local copies, waits for them, and re-layouts  1.59 us (1%)
    ppermute x20, starting transfers between devices, passed_along(): lax.ppermute(value, axis, [(source, source + steps) for source in range(f...  61.1 us
    psum x1, waiting for transfers between devices, shards(): first, second = lax.psum((pressure, pressure * pressure), 'shift')  35.9 us
    ppermute x20, waiting for transfers between devices, passed_along(): lax.ppermute(value, axis, [(source, source + steps) for source in range(f...  9.4 us
    all_to_all x1, starting transfers between devices, shards(): lax.all_to_all(outgoing, 'space', split_axis=0, concat_axis=1, tiled=True)  7.25 us
    all_to_all x1, waiting for transfers between devices, shards(): lax.all_to_all(outgoing, 'space', split_axis=0, concat_axis=1, tiled=True)  6.83 us
    dot_general x1, matrix products, shards(): jnp.dot(pencils[1], jnp.sin(angle), precision=lax.Precision.HIGHEST, pref...  3.02 us
  transfers between devices with their start and end apart: 22, of which 7 were waited for; matrix products, arithmetic and copies ran while one was open for 0% of the time, Pallas kernels for 0%

commit v1 on v0

--- a/solution.py
+++ b/solution.py
@@ -1,11 +1,21 @@
+import functools
 import math
 
 import jax
 import jax.numpy as jnp
+import ml_dtypes
+import numpy as np
 from jax import lax
+from jax.experimental import pallas as pl
+from jax.experimental.pallas import tpu as pltpu
 from jax.sharding import PartitionSpec as P
 
 ITERS = 4
+MESH = pl.DeviceIdType.MESH
+SLABS = 8
+SLAB = 32
+MARGIN = 16
+QUARTERS = 4
 
 
 reaction = 0.02
@@ -151,7 +161,320 @@
     return (pressure_mean[None], pressure_variance[None])
 
 
+def lanes_of(value):
+    return lax.broadcasted_iota(jnp.int32, value.shape, value.ndim - 1)
+
+
+def roll_lanes(value, shift):
+    shift = shift % value.shape[-1]
+    return pltpu.roll(value, shift, value.ndim - 1) if shift else value
+
+
+def window(low, high, slab, offset):
+    start = (SLAB * slab - MARGIN) % 128
+    shift = 128 - start + offset
+    begin = SLAB * slab - MARGIN
+    if begin + 64 <= 128 or slab == 0:
+        return roll_lanes(low, shift)
+    if begin >= 128:
+        return roll_lanes(high, shift)
+    return jnp.where(
+        lanes_of(low) < 128 - start + offset, roll_lanes(low, shift), roll_lanes(high, shift)
+    )
+
+
+def window_pair(first, second, slab):
+    left = window(first[..., :128], first[..., 128:], slab, 0)
+    right = window(second[..., :128], second[..., 128:], slab, 64)
+    return jnp.where(lanes_of(left) < 64, left, right)
+
+
+def slab_kernel(
+    coef_ref, source_ref, table_hbm,
+    mean_ref, var_ref,
+    table, src_send, src_recv, perm_send, perm_recv, w_x, w_y, w_z, rdiag, resid, direc, press,
+    part_send, part_recv, brick_send, brick_recv,
+    table_sem, src_ss, src_rs, perm_ss, perm_rs, part_ss, part_rs, brick_ss, brick_rs,
+):
+    shift = lax.axis_index("shift")
+    me = lax.axis_index("space")
+    by = lax.rem(me, QUARTERS)
+    own = by == shift
+
+    table_copy = pltpu.make_async_copy(table_hbm, table, table_sem)
+    table_copy.start()
+
+    barrier = pltpu.get_barrier_semaphore()
+    for step in range(1, SLABS):
+        pl.semaphore_signal(
+            barrier, inc=1, device_id={"space": lax.rem(me + step, SLABS)}, device_id_type=MESH
+        )
+    for step in range(1, QUARTERS):
+        pl.semaphore_signal(
+            barrier, inc=1, device_id={"shift": lax.rem(shift + step, QUARTERS)}, device_id_type=MESH
+        )
+    for slab in range(SLABS):
+
+        @pl.when(jnp.logical_not(jnp.logical_and(own, me == slab)))
+        def _():
+            pl.semaphore_signal(
+                barrier, inc=1, device_id={"shift": by, "space": slab}, device_id_type=MESH
+            )
+
+    for slab in range(SLABS):
+        for row in range(4):
+            src_send[slab, row] = window_pair(source_ref[row], source_ref[row + 4], slab)
+
+    pl.semaphore_wait(barrier, SLABS - 1 + QUARTERS - 1 + SLABS - own.astype(jnp.int32))
+
+    def space_copy(send, recv, ss, rs, slot, target):
+        return pltpu.make_async_remote_copy(
+            src_ref=send.at[target], dst_ref=recv.at[slot], send_sem=ss.at[target],
+            recv_sem=rs.at[slot], device_id={"space": target}, device_id_type=MESH,
+        )
+
+    for step in range(1, SLABS):
+        space_copy(src_send, src_recv, src_ss, src_rs, me, lax.rem(me + step, SLABS)).start()
+    src_recv[me] = src_send[me]
+
+    real, imag = coef_ref[0], coef_ref[1]
+    real_hi, imag_hi = real.astype(jnp.bfloat16), imag.astype(jnp.bfloat16)
+    real_lo = (real - real_hi.astype(jnp.float32)).astype(jnp.bfloat16)
+    imag_lo = (imag - imag_hi.astype(jnp.float32)).astype(jnp.bfloat16)
+    table_copy.wait()
+    dot = functools.partial(jnp.dot, preferred_element_type=jnp.float32)
+    rows = real.shape[0]
+    both = dot(jnp.concatenate([real_hi, real_lo], 0), table[0, 0])
+    both = both + dot(jnp.concatenate([imag_hi, imag_lo], 0), table[0, 1])
+    rest = dot(real_hi, table[1, 0]) + dot(imag_hi, table[1, 1])
+    perm = jnp.exp(both[:rows] + (both[rows:] + rest))
+    half = rows // 2
+    for slab in range(SLABS):
+        perm_send[slab] = window_pair(perm[:half], perm[half:], slab)
+    for step in range(1, SLABS):
+        space_copy(perm_send, perm_recv, perm_ss, perm_rs, me, lax.rem(me + step, SLABS)).start()
+    perm_recv[me] = perm_send[me]
+
+    for step in range(1, SLABS):
+        slot = lax.rem(me + step, SLABS)
+        space_copy(perm_send, perm_recv, perm_ss, perm_rs, slot, slot).wait_recv()
+
+    shape = (32, 128)
+    lane = lax.broadcasted_iota(jnp.int32, shape, 1)
+    sub = lax.broadcasted_iota(jnp.int32, shape, 0)
+    place = SLAB * me - MARGIN + lax.rem(lane, 64)
+    inner_z = jnp.logical_and(place != -1, place != 255)
+    inner_y = sub != 31
+    inner_x = lane < 64
+
+    def next_y(value):
+        return pltpu.roll(value, 31, 0)
+
+    def last_y(value):
+        return pltpu.roll(value, 1, 0)
+
+    def next_z(value):
+        return roll_lanes(value, 127)
+
+    def last_z(value):
+        return roll_lanes(value, 1)
+
+    def face_x(n):
+        upper = roll_lanes(perm_recv[0], 64) if n == 7 else perm_recv[n + 1]
+        weight = harmonic(perm_recv[n], upper)
+        return jnp.where(inner_x, weight, 0.0) if n == 7 else weight
+
+    last = face_x(7)
+    w_x[7] = last
+    lower_x = roll_lanes(last, 64)
+    for n in range(8):
+        cell = perm_recv[n]
+        if n < 7:
+            last = face_x(n)
+            w_x[n] = last
+        else:
+            last = w_x[7]
+        up_y = jnp.where(inner_y, harmonic(cell, next_y(cell)), 0.0)
+        up_z = jnp.where(inner_z, harmonic(cell, next_z(cell)), 0.0)
+        w_y[n] = up_y
+        w_z[n] = up_z
+        diagonal = reaction + (lower_x + last) + (last_y(up_y) + up_y) + (last_z(up_z) + up_z)
+        rdiag[n] = 1.0 / diagonal
+        lower_x = last
+
+    for step in range(1, SLABS):
+        slot = lax.rem(me + step, SLABS)
+        space_copy(src_send, src_recv, src_ss, src_rs, slot, slot).wait_recv()
+    left8 = lax.broadcasted_iota(jnp.int32, (8, 128), 1) < 64
+    for n in range(8):
+        for brick_y in range(QUARTERS):
+            near, far = src_recv[brick_y, n % 4], src_recv[QUARTERS + brick_y, n % 4]
+            if n < 4:
+                far = roll_lanes(far, 64)
+            else:
+                near = roll_lanes(near, 64)
+            piece = jnp.where(left8, near, far)
+            rows_y = slice(brick_y * 8, brick_y * 8 + 8)
+            resid[n, rows_y] = piece
+            direc[n, rows_y] = piece * rdiag[n, rows_y] * (1.0 / centre)
+
+    ratio_now = 1.0 / sigma_one
+    for sweep in range(ITERS):
+        ratio_next = 1.0 / (2.0 * sigma_one - ratio_now)
+        keep, gain = ratio_next * ratio_now, 2.0 * ratio_next / half_width
+        ratio_now = ratio_next
+        first_next = roll_lanes(direc[0], 64)
+        flux_last = w_x[7] * (direc[7] - first_next)
+        lower_flux = roll_lanes(flux_last, 64)
+        for n in range(8):
+            now = direc[n]
+            flux = w_x[n] * (now - direc[n + 1]) if n < 7 else flux_last
+            flux_y = w_y[n] * (now - next_y(now))
+            flux_z = w_z[n] * (now - next_z(now))
+            total = reaction * now + (flux - lower_flux)
+            total = total + (flux_y - last_y(flux_y)) + (flux_z - last_z(flux_z))
+            lower_flux = flux
+            left_over = resid[n] - total
+            if sweep < ITERS - 1:
+                resid[n] = left_over
+            new = keep * now + gain * (left_over * rdiag[n])
+            so_far = now + press[n] if sweep else now
+            if sweep < ITERS - 1:
+                direc[n] = new
+                press[n] = so_far
+            else:
+                press[n] = so_far + new
+
+    even = lax.rem(lane // 32, 2) == 0
+    for row in range(4):
+        packed = jnp.where(even, roll_lanes(press[row], -MARGIN), roll_lanes(press[row + 4], MARGIN))
+        for quarter in range(QUARTERS):
+            part_send[quarter, row] = packed[quarter * 8 : quarter * 8 + 8]
+
+    def part_copy(slot, target):
+        return pltpu.make_async_remote_copy(
+            src_ref=part_send.at[target], dst_ref=part_recv.at[slot], send_sem=part_ss.at[target],
+            recv_sem=part_rs.at[slot], device_id={"shift": target}, device_id_type=MESH,
+        )
+
+    for step in range(1, QUARTERS):
+        part_copy(shift, lax.rem(shift + step, QUARTERS)).start()
+    part_recv[shift] = part_send[shift]
+    for step in range(1, QUARTERS):
+        slot = lax.rem(shift + step, QUARTERS)
+        part_copy(slot, slot).wait_recv()
+
+    for row in range(4):
+        parts = [part_recv[slot, row] for slot in range(QUARTERS)]
+        first = (parts[0] + parts[1]) + (parts[2] + parts[3])
+        second = (parts[0] * parts[0] + parts[1] * parts[1]) + (parts[2] * parts[2] + parts[3] * parts[3])
+        mean = first * (1.0 / QUARTERS)
+        var = (second - first * mean) * (1.0 / (QUARTERS - 1))
+        brick_send[0, row] = jnp.where(left8, mean, roll_lanes(var, 64))
+        brick_send[1, row] = jnp.where(left8, roll_lanes(mean, 64), var)
+
+    def brick_copy(bx, step, slot):
+        return pltpu.make_async_remote_copy(
+            src_ref=brick_send.at[bx], dst_ref=brick_recv.at[slot],
+            send_sem=brick_ss.at[bx * QUARTERS + step], recv_sem=brick_rs.at[slot],
+            device_id={"shift": lax.rem(shift + step, QUARTERS), "space": bx * QUARTERS + shift},
+            device_id_type=MESH,
+        )
+
+    for step in range(QUARTERS):
+        for bx in range(2):
+            if step:
+                brick_copy(bx, step, me).start()
+            else:
+
+                @pl.when(me != bx * QUARTERS + shift)
+                def _():
+                    brick_copy(bx, step, me).start()
+
+    @pl.when(own)
+    def _():
+        brick_recv[me] = brick_send[me // QUARTERS]
+
+    for slab in range(SLABS):
+
+        @pl.when(jnp.logical_not(jnp.logical_and(own, me == slab)))
+        def _():
+            brick_copy(0, 1, slab).wait_recv()
+
+    group = lax.broadcasted_iota(jnp.int32, (8, 128), 1) // 32
+    for which, out_ref in enumerate((mean_ref, var_ref)):
+        for high in range(2):
+            place_in = which * 2 + high
+            for row in range(4):
+                for side in range(2):
+                    done = None
+                    for lap in range(4):
+                        piece = roll_lanes(brick_recv[side * 4 + lap, row], 32 * (lap - place_in))
+                        done = piece if done is None else jnp.where(group == lap, piece, done)
+                    out_ref[high * 4 + row, :, side * 128 : side * 128 + 128] = done
+
+    for step in range(1, SLABS):
+        target = lax.rem(me + step, SLABS)
+        space_copy(src_send, src_recv, src_ss, src_rs, target, target).wait_send()
+        space_copy(perm_send, perm_recv, perm_ss, perm_rs, target, target).wait_send()
+    for step in range(1, QUARTERS):
+        target = lax.rem(shift + step, QUARTERS)
+        part_copy(target, target).wait_send()
+    for step in range(QUARTERS):
+        for bx in range(2):
+            if step:
+                brick_copy(bx, step, me).wait_send()
+            else:
+
+                @pl.when(me != bx * QUARTERS + shift)
+                def _():
+                    brick_copy(bx, step, me).wait_send()
+
+
+def slab_shards(coefficients, source):
+    modes_count = coefficients.shape[-1]
+    cells_z = modes_count // 2
+    angle = 2.0 * np.pi / modes_count * (np.outer(np.arange(modes_count), np.arange(cells_z)) % modes_count)
+    exact = np.stack([np.cos(angle), np.sin(angle)])
+    high = exact.astype(ml_dtypes.bfloat16)
+    low = (exact - high.astype(np.float64)).astype(ml_dtypes.bfloat16)
+    table = jnp.asarray(np.stack([high, low]))
+    f32 = jnp.float32
+    field = pltpu.VMEM((8, 32, 128), f32)
+    vmem = pl.BlockSpec(memory_space=pltpu.VMEM)
+    dma = pltpu.SemaphoreType.DMA
+    out = jax.ShapeDtypeStruct((8, 8, cells_z), f32)
+    mean, var = pl.pallas_call(
+        slab_kernel,
+        out_shape=(out, out),
+        in_specs=[vmem, vmem, pl.BlockSpec(memory_space=pl.ANY)],
+        out_specs=(vmem, vmem),
+        scratch_shapes=[
+            pltpu.VMEM(table.shape, jnp.bfloat16),
+            pltpu.VMEM((8, 4, 8, 128), f32), pltpu.VMEM((8, 4, 8, 128), f32),
+            field, field, field, field, field, field, field, field, field,
+            pltpu.VMEM((4, 4, 8, 128), f32), pltpu.VMEM((4, 4, 8, 128), f32),
+            pltpu.VMEM((2, 4, 8, 128), f32), pltpu.VMEM((8, 4, 8, 128), f32),
+            dma, dma((8,)), dma((8,)), dma((8,)), dma((8,)), dma((4,)), dma((4,)), dma((8,)), dma((8,)),
+        ],
+        compiler_params=pltpu.CompilerParams(
+            collective_id=0, has_side_effects=True, vmem_limit_bytes=32 * 1024 * 1024
+        ),
+    )(coefficients.reshape(2, 64, modes_count), source[0], table)
+    return mean[None], var[None]
+
+
 def solution(mesh):
     in_specs = (P("shift", None, None, "space", None, None), P("space", None, None, None))
     out_specs = (P("space", None, None, None), P("space", None, None, None))
-    return jax.shard_map(shards, mesh=mesh, in_specs=in_specs, out_specs=out_specs, check_vma=False)
+
+    def chosen(coefficients, source):
+        slabs = (
+            coefficients.shape == (1, 2, 2, 1, 32, 512)
+            and source.shape == (1, 8, 8, 256)
+            and mesh.shape["space"] == SLABS
+            and mesh.shape["shift"] == QUARTERS
+        )
+        return slab_shards(coefficients, source) if slabs else shards(coefficients, source)
+
+    return jax.shard_map(chosen, mesh=mesh, in_specs=in_specs, out_specs=out_specs, check_vma=False)

time: 146 us -> 29 us (0.20)
  starting transfers between devices: 68.4 us -> 0 us
  waiting for transfers between devices: 52.1 us -> 0 us
  Pallas kernels: 0 us -> 23.6 us
  between operations: 14.6 us -> 0.65 us
  matrix products: 5.39 us -> 0 us
  other arithmetic: 2.95 us -> 0 us
  local copies, waits for them, and re-layouts: 1.59 us -> 4.27 us
    ppermute x20 -> x0, starting transfers between devices: 61.1 us -> none  [passed_along(): lax.ppermute(value, axis, [(source, source + steps) for source in range(f...]
    psum x1 -> x0, waiting for transfers between devices: 35.9 us -> none  [shards(): first, second = lax.psum((pressure, pressure * pressure), 'shift')]
    pallas_call x0 -> x1, Pallas kernels: none -> 23.6 us  [slab_shards(): pl.pallas_call(slab_kernel, out_shape=(out, out), in_specs=[vmem, vmem, p...]
    ppermute x20 -> x0, waiting for transfers between devices: 9.4 us -> none  [passed_along(): lax.ppermute(value, axis, [(source, source + steps) for source in range(f...]
    all_to_all x1 -> x0, starting transfers between devices: 7.25 us -> none  [shards(): lax.all_to_all(outgoing, 'space', split_axis=0, concat_axis=1, tiled=True)]
    all_to_all x1 -> x0, waiting for transfers between devices: 6.83 us -> none  [shards(): lax.all_to_all(outgoing, 'space', split_axis=0, concat_axis=1, tiled=True)]
    dot_general x2 -> x0, matrix products: 5.39 us -> none  [the longest x1 3.02 us: shards(): jnp.dot(pencils[1], jnp.sin(angle), precision=lax.Precision.HIGHEST, pref...]
    unnamed x2 -> x8, local copies, waits for them, and re-layouts: 0.01 us -> 4.27 us
  transfers between devices with their start and end apart: 22 -> 0, of which waited for: 7 -> 0; matrix products, arithmetic and copies ran while one was open for 0% -> 0% of each run, Pallas kernels for 0% -> 0%
where the time goes in v1:
time: 29 us; the launch traced here: 28.5 us
  Pallas kernels  23.6 us (81%)
  local copies, waits for them, and re-layouts  4.27 us (15%)
  between operations  0.65 us (2%)
    pallas_call x1, Pallas kernels, slab_shards(): pl.pallas_call(slab_kernel, out_shape=(out, out), in_specs=[vmem, vmem, p...  23.6 us
    unnamed x8, local copies, waits for them, and re-layouts  4.27 us

profile of v1, /device:TPU:0, one launch (start us, length us, event | category | flops | bytes accessed | tf_op | source)
XLA Modules:
  0.0 28.5 jit_solution(9578437188864187055)
XLA Ops:
  0.6 0.0 copy-start
  0.6 1.2 %copy-done = bf16[2,2,512,256]{3,2,1,0:T(8,128)(2,1)S(1)} copy-done((bf16[2,2,512,256]{3,2,1,0:T(8,128)(2,1)S(1)}, bf16[2,2,512,256]{3,2,1,0:T(8,128)(2,1)}, u32[]{:S(2)}) %copy-start) | copy-done | bytes 1048600
  1.9 0.0 copy-start.1
  1.9 0.9 %copy-done.1 = f32[1,2,2,1,32,512]{5,4,3,2,1,0:T(8,128)S(1)} copy-done((f32[1,2,2,1,32,512]{5,4,3,2,1,0:T(8,128)S(1)}, f32[1,2,2,1,32,512]{5,4,3,2,1,0:T(8,128)}, u32[]{:S(2)}) %copy-start.1) | copy-done | bytes 262168
  2.8 0.0 copy-start.2
  2.8 0.8 %copy-done.2 = f32[1,8,8,256]{3,2,1,0:T(8,128)S(1)} copy-done((f32[1,8,8,256]{3,2,1,0:T(8,128)S(1)}, f32[1,8,8,256]{3,2,1,0:T(8,128)}, u32[]{:S(2)}) %copy-start.2) | copy-done | bytes 65560
  3.6 23.6 %shard_map.50 = (f32[8,8,256]{2,1,0:T(8,128)S(1)}, f32[8,8,256]{2,1,0:T(8,128)S(1)}) custom-call(f32[2,64,512]{2,1,0:T(8,128)S(1)} %bitcast.4, f32[8,8,256]{2,1,0:T(8,128)S(1)} %bitcast.7, bf16[2,2,512,256]{3,2,1,0:T(8,128)(2,1)S(1)} %copy-done), custom_call_target="tpu_custom_call" | custom-call | tf_op jit(solution)/shard_map/pallas_call | solution.py:447
  27.3 0.6 %copy.7 = f32[1,8,8,256]{3,2,1,0:T(8,128)} copy(f32[1,8,8,256]{3,2,1,0:T(8,128)S(1)} %bitcast.6) | data formatting | bytes 131072
  27.9 0.6 %copy.8 = f32[1,8,8,256]{3,2,1,0:T(8,128)} copy(f32[1,8,8,256]{3,2,1,0:T(8,128)S(1)} %bitcast.5) | data formatting | bytes 131072
Async XLA Ops:
  0.6 1.2 %copy-start = (bf16[2,2,512,256]{3,2,1,0:T(8,128)(2,1)S(1)}, bf16[2,2,512,256]{3,2,1,0:T(8,128)(2,1)}, u32[]{:S(2)}) copy-start(bf16[2,2,512,256]{3,2,1,0:T(8,128)(2,1)} %constant.2.clone.table_hbm) | copy-start | bytes 3145732
  1.9 0.9 %copy-start.1 = (f32[1,2,2,1,32,512]{5,4,3,2,1,0:T(8,128)S(1)}, f32[1,2,2,1,32,512]{5,4,3,2,1,0:T(8,128)}, u32[]{:S(2)}) copy-start(f32[1,2,2,1,32,512]{5,4,3,2,1,0:T(8,128)} %param.3) | copy-start | bytes 786436
  2.8 0.8 %copy-start.2 = (f32[1,8,8,256]{3,2,1,0:T(8,128)S(1)}, f32[1,8,8,256]{3,2,1,0:T(8,128)}, u32[]{:S(2)}) copy-start(f32[1,8,8,256]{3,2,1,0:T(8,128)} %param.4) | copy-start | bytes 196612

commit v2 on v1

--- a/solution.py
+++ b/solution.py
@@ -190,42 +190,49 @@
 
 
 def slab_kernel(
-    coef_ref, source_ref, table_hbm,
-    mean_ref, var_ref,
-    table, src_send, src_recv, perm_send, perm_recv, w_x, w_y, w_z, rdiag, resid, direc, press,
-    part_send, part_recv, brick_send, brick_recv,
-    table_sem, src_ss, src_rs, perm_ss, perm_rs, part_ss, part_rs, brick_ss, brick_rs,
+    coef_hbm, source_hbm, table_hbm,
+    moment_ref,
+    coef_ref, source_ref, table, src_send, src_recv, perm_send, perm_recv, w_x, w_y, w_z, rdiag, resid, direc, press,
+    part_send, part_recv,
+    source_sem, coef_sem, table_sem, src_ss, src_rs, share_ss, share_rs, perm_ss, perm_rs,
+    part_ss, part_rs, hand_ss, hand_rs,
 ):
     shift = lax.axis_index("shift")
     me = lax.axis_index("space")
-    by = lax.rem(me, QUARTERS)
-    own = by == shift
-
+    side_y, core = shift // 2, lax.rem(shift, 2)
+    partner = 2 * side_y + (1 - core)
+    across = 2 * (1 - side_y) + core
+
+    source_copies = [
+        pltpu.make_async_copy(source_hbm.at[shift + 4 * half], source_ref.at[half], source_sem.at[half])
+        for half in range(2)
+    ]
+    coef_copy = pltpu.make_async_copy(coef_hbm, coef_ref, coef_sem)
     table_copy = pltpu.make_async_copy(table_hbm, table, table_sem)
-    table_copy.start()
+    for copy in (*source_copies, coef_copy, table_copy):
+        copy.start()
 
     barrier = pltpu.get_barrier_semaphore()
-    for step in range(1, SLABS):
+
+    def greet(to_shift, to_space):
         pl.semaphore_signal(
-            barrier, inc=1, device_id={"space": lax.rem(me + step, SLABS)}, device_id_type=MESH
-        )
-    for step in range(1, QUARTERS):
-        pl.semaphore_signal(
-            barrier, inc=1, device_id={"shift": lax.rem(shift + step, QUARTERS)}, device_id_type=MESH
-        )
+            barrier, inc=1, device_id={"shift": to_shift, "space": to_space}, device_id_type=MESH
+        )
+
+    for step in range(SLABS):
+        other = lax.rem(me + step, SLABS)
+        if step:
+            greet(shift, other)
+        greet(across, other)
+    greet(partner, me)
+    greet(2 * (1 - side_y) + (1 - core), me)
+
+    for copy in source_copies:
+        copy.wait()
     for slab in range(SLABS):
-
-        @pl.when(jnp.logical_not(jnp.logical_and(own, me == slab)))
-        def _():
-            pl.semaphore_signal(
-                barrier, inc=1, device_id={"shift": by, "space": slab}, device_id_type=MESH
-            )
-
-    for slab in range(SLABS):
-        for row in range(4):
-            src_send[slab, row] = window_pair(source_ref[row], source_ref[row + 4], slab)
-
-    pl.semaphore_wait(barrier, SLABS - 1 + QUARTERS - 1 + SLABS - own.astype(jnp.int32))
+        src_send[slab] = window_pair(source_ref[0], source_ref[1], slab)
+
+    pl.semaphore_wait(barrier, 2 * SLABS + 1)
 
     def space_copy(send, recv, ss, rs, slot, target):
         return pltpu.make_async_remote_copy(
@@ -233,10 +240,23 @@
             recv_sem=rs.at[slot], device_id={"space": target}, device_id_type=MESH,
         )
 
+    def source_copy(slot, target):
+        return pltpu.make_async_remote_copy(
+            src_ref=src_send.at[target], dst_ref=src_recv.at[shift, slot], send_sem=src_ss.at[target],
+            recv_sem=src_rs.at[slot], device_id={"space": target}, device_id_type=MESH,
+        )
+
+    def share_copy(slot, target):
+        return pltpu.make_async_remote_copy(
+            src_ref=src_recv.at[slot], dst_ref=src_recv.at[slot], send_sem=share_ss.at[target],
+            recv_sem=share_rs.at[slot], device_id={"shift": target}, device_id_type=MESH,
+        )
+
     for step in range(1, SLABS):
-        space_copy(src_send, src_recv, src_ss, src_rs, me, lax.rem(me + step, SLABS)).start()
-    src_recv[me] = src_send[me]
-
+        source_copy(me, lax.rem(me + step, SLABS)).start()
+    src_recv[shift, me] = src_send[me]
+
+    coef_copy.wait()
     real, imag = coef_ref[0], coef_ref[1]
     real_hi, imag_hi = real.astype(jnp.bfloat16), imag.astype(jnp.bfloat16)
     real_lo = (real - real_hi.astype(jnp.float32)).astype(jnp.bfloat16)
@@ -257,6 +277,12 @@
 
     for step in range(1, SLABS):
         slot = lax.rem(me + step, SLABS)
+        source_copy(slot, slot).wait_recv()
+    for step in range(1, QUARTERS):
+        share_copy(shift, lax.rem(shift + step, QUARTERS)).start()
+
+    for step in range(1, SLABS):
+        slot = lax.rem(me + step, SLABS)
         space_copy(perm_send, perm_recv, perm_ss, perm_rs, slot, slot).wait_recv()
 
     shape = (32, 128)
@@ -302,13 +328,13 @@
         rdiag[n] = 1.0 / diagonal
         lower_x = last
 
-    for step in range(1, SLABS):
-        slot = lax.rem(me + step, SLABS)
-        space_copy(src_send, src_recv, src_ss, src_rs, slot, slot).wait_recv()
+    for step in range(1, QUARTERS):
+        slot = lax.rem(shift + step, QUARTERS)
+        share_copy(slot, slot).wait_recv()
     left8 = lax.broadcasted_iota(jnp.int32, (8, 128), 1) < 64
     for n in range(8):
         for brick_y in range(QUARTERS):
-            near, far = src_recv[brick_y, n % 4], src_recv[QUARTERS + brick_y, n % 4]
+            near, far = src_recv[n % 4, brick_y], src_recv[n % 4, QUARTERS + brick_y]
             if n < 4:
                 far = roll_lanes(far, 64)
             else:
@@ -345,90 +371,81 @@
             else:
                 press[n] = so_far + new
 
-    even = lax.rem(lane // 32, 2) == 0
-    for row in range(4):
-        packed = jnp.where(even, roll_lanes(press[row], -MARGIN), roll_lanes(press[row + 4], MARGIN))
-        for quarter in range(QUARTERS):
-            part_send[quarter, row] = packed[quarter * 8 : quarter * 8 + 8]
-
-    def part_copy(slot, target):
+    group = lane // 32
+    for bx in range(2):
+        for tile in range(2):
+            packed = None
+            for quad in range(4):
+                piece = roll_lanes(press[quad * 2 + tile], 32 * quad - 64 * bx - MARGIN)
+                packed = piece if packed is None else jnp.where(group == quad, piece, packed)
+            for brick_y in range(QUARTERS):
+                part_send[bx * QUARTERS + brick_y, tile] = packed[brick_y * 8 : brick_y * 8 + 8]
+
+    def part_copy(from_shift, from_slab, to_side, to_shift, target):
         return pltpu.make_async_remote_copy(
-            src_ref=part_send.at[target], dst_ref=part_recv.at[slot], send_sem=part_ss.at[target],
-            recv_sem=part_rs.at[slot], device_id={"shift": target}, device_id_type=MESH,
-        )
-
-    for step in range(1, QUARTERS):
-        part_copy(shift, lax.rem(shift + step, QUARTERS)).start()
-    part_recv[shift] = part_send[shift]
-    for step in range(1, QUARTERS):
-        slot = lax.rem(shift + step, QUARTERS)
-        part_copy(slot, slot).wait_recv()
-
-    for row in range(4):
-        parts = [part_recv[slot, row] for slot in range(QUARTERS)]
-        first = (parts[0] + parts[1]) + (parts[2] + parts[3])
-        second = (parts[0] * parts[0] + parts[1] * parts[1]) + (parts[2] * parts[2] + parts[3] * parts[3])
-        mean = first * (1.0 / QUARTERS)
-        var = (second - first * mean) * (1.0 / (QUARTERS - 1))
-        brick_send[0, row] = jnp.where(left8, mean, roll_lanes(var, 64))
-        brick_send[1, row] = jnp.where(left8, roll_lanes(mean, 64), var)
-
-    def brick_copy(bx, step, slot):
+            src_ref=part_send.at[target], dst_ref=part_recv.at[from_shift, from_slab],
+            send_sem=part_ss.at[to_side, target], recv_sem=part_rs.at[from_shift, from_slab],
+            device_id={"shift": to_shift, "space": target}, device_id_type=MESH,
+        )
+
+    def hand_copy(of_shift, half):
+        part = part_recv.at[of_shift, pl.ds(4 * half, 4)]
         return pltpu.make_async_remote_copy(
-            src_ref=brick_send.at[bx], dst_ref=brick_recv.at[slot],
-            send_sem=brick_ss.at[bx * QUARTERS + step], recv_sem=brick_rs.at[slot],
-            device_id={"shift": lax.rem(shift + step, QUARTERS), "space": bx * QUARTERS + shift},
-            device_id_type=MESH,
-        )
-
-    for step in range(QUARTERS):
-        for bx in range(2):
-            if step:
-                brick_copy(bx, step, me).start()
-            else:
-
-                @pl.when(me != bx * QUARTERS + shift)
-                def _():
-                    brick_copy(bx, step, me).start()
-
-    @pl.when(own)
-    def _():
-        brick_recv[me] = brick_send[me // QUARTERS]
-
-    for slab in range(SLABS):
-
-        @pl.when(jnp.logical_not(jnp.logical_and(own, me == slab)))
-        def _():
-            brick_copy(0, 1, slab).wait_recv()
+            src_ref=part, dst_ref=part, send_sem=hand_ss.at[of_shift, half],
+            recv_sem=hand_rs.at[of_shift, half], device_id={"shift": partner}, device_id_type=MESH,
+        )
+
+    for step in range(SLABS):
+        target = lax.rem(me + step, SLABS)
+        if step:
+            part_copy(shift, me, 0, shift, target).start()
+        part_copy(shift, me, 1, across, target).start()
+    part_recv[shift, me] = part_send[me]
+
+    for of_shift in (shift, across):
+        for half in range(2):
+            for slab in range(half * 4, half * 4 + 4):
+                if of_shift is shift:
+
+                    @pl.when(me != slab)
+                    def _():
+                        part_copy(shift, slab, 0, shift, slab).wait_recv()
+                else:
+                    part_copy(across, slab, 1, across, slab).wait_recv()
+            hand_copy(of_shift, half).start()
+    for of_side in range(2):
+        for half in range(2):
+            hand_copy(2 * of_side + (1 - core), half).wait_recv()
 
     group = lax.broadcasted_iota(jnp.int32, (8, 128), 1) // 32
-    for which, out_ref in enumerate((mean_ref, var_ref)):
-        for high in range(2):
-            place_in = which * 2 + high
-            for row in range(4):
-                for side in range(2):
+    for tile in range(2):
+        for side in range(2):
+            sums = [[], []]
+            for lap in range(4):
+                parts = [part_recv[slot, side * 4 + lap, tile] for slot in range(QUARTERS)]
+                sums[0].append((parts[0] + parts[1]) + (parts[2] + parts[3]))
+                squares = [part * part for part in parts]
+                sums[1].append((squares[0] + squares[1]) + (squares[2] + squares[3]))
+            for which in range(2):
+                for quad in range(4):
                     done = None
                     for lap in range(4):
-                        piece = roll_lanes(brick_recv[side * 4 + lap, row], 32 * (lap - place_in))
+                        piece = roll_lanes(sums[which][lap], 32 * (lap - quad))
                         done = piece if done is None else jnp.where(group == lap, piece, done)
-                    out_ref[high * 4 + row, :, side * 128 : side * 128 + 128] = done
-
-    for step in range(1, SLABS):
+                    moment_ref[which, quad * 2 + tile, :, side * 128 : side * 128 + 128] = done
+
+    for step in range(SLABS):
         target = lax.rem(me + step, SLABS)
-        space_copy(src_send, src_recv, src_ss, src_rs, target, target).wait_send()
-        space_copy(perm_send, perm_recv, perm_ss, perm_rs, target, target).wait_send()
+        if step:
+            source_copy(target, target).wait_send()
+            space_copy(perm_send, perm_recv, perm_ss, perm_rs, target, target).wait_send()
+            part_copy(shift, me, 0, shift, target).wait_send()
+        part_copy(shift, me, 1, across, target).wait_send()
     for step in range(1, QUARTERS):
-        target = lax.rem(shift + step, QUARTERS)
-        part_copy(target, target).wait_send()
-    for step in range(QUARTERS):
-        for bx in range(2):
-            if step:
-                brick_copy(bx, step, me).wait_send()
-            else:
-
-                @pl.when(me != bx * QUARTERS + shift)
-                def _():
-                    brick_copy(bx, step, me).wait_send()
+        share_copy(shift, lax.rem(shift + step, QUARTERS)).wait_send()
+    for of_shift in (shift, across):
+        for half in range(2):
+            hand_copy(of_shift, half).wait_send()
 
 
 def slab_shards(coefficients, source):
@@ -441,26 +458,29 @@
     table = jnp.asarray(np.stack([high, low]))
     f32 = jnp.float32
     field = pltpu.VMEM((8, 32, 128), f32)
-    vmem = pl.BlockSpec(memory_space=pltpu.VMEM)
     dma = pltpu.SemaphoreType.DMA
-    out = jax.ShapeDtypeStruct((8, 8, cells_z), f32)
-    mean, var = pl.pallas_call(
+    anywhere = pl.BlockSpec(memory_space=pl.ANY)
+    moments = pl.pallas_call(
         slab_kernel,
-        out_shape=(out, out),
-        in_specs=[vmem, vmem, pl.BlockSpec(memory_space=pl.ANY)],
-        out_specs=(vmem, vmem),
+        out_shape=jax.ShapeDtypeStruct((2, 8, 8, cells_z), f32),
+        in_specs=[anywhere, anywhere, anywhere],
+        out_specs=pl.BlockSpec(memory_space=pltpu.VMEM),
         scratch_shapes=[
+            pltpu.VMEM((2, 64, modes_count), f32), pltpu.VMEM((2, 8, cells_z), f32),
             pltpu.VMEM(table.shape, jnp.bfloat16),
-            pltpu.VMEM((8, 4, 8, 128), f32), pltpu.VMEM((8, 4, 8, 128), f32),
+            pltpu.VMEM((8, 8, 128), f32), pltpu.VMEM((4, 8, 8, 128), f32),
             field, field, field, field, field, field, field, field, field,
-            pltpu.VMEM((4, 4, 8, 128), f32), pltpu.VMEM((4, 4, 8, 128), f32),
-            pltpu.VMEM((2, 4, 8, 128), f32), pltpu.VMEM((8, 4, 8, 128), f32),
-            dma, dma((8,)), dma((8,)), dma((8,)), dma((8,)), dma((4,)), dma((4,)), dma((8,)), dma((8,)),
+            pltpu.VMEM((8, 2, 8, 128), f32), pltpu.VMEM((4, 8, 2, 8, 128), f32),
+            dma((2,)), dma, dma, dma((8,)), dma((8,)), dma((4,)), dma((4,)), dma((8,)), dma((8,)),
+            dma((2, 8)), dma((4, 8)), dma((4, 2)), dma((4, 2)),
         ],
         compiler_params=pltpu.CompilerParams(
-            collective_id=0, has_side_effects=True, vmem_limit_bytes=32 * 1024 * 1024
+            collective_id=0, has_side_effects=True, vmem_limit_bytes=56 * 1024 * 1024
         ),
     )(coefficients.reshape(2, 64, modes_count), source[0], table)
+    first, second = moments[0], moments[1]
+    mean = first / QUARTERS
+    var = (second - first * mean) / (QUARTERS - 1)
     return mean[None], var[None]
 
 

time: 29 us -> 24.8 us (0.86)
  local copies, waits for them, and re-layouts: 4.27 us -> 0 us
  other arithmetic: 0 us -> 1.53 us
  Pallas kernels: 23.6 us -> 22.3 us
    unnamed x8 -> x0, local copies, waits for them, and re-layouts: 4.27 us -> none
    div x0 -> x1, other arithmetic: none -> 1.53 us  [slab_shards(): var = (second - first * mean) / (QUARTERS - 1)]
    pallas_call x1, Pallas kernels: 23.6 us -> 22.3 us  [slab_shards(): pl.pallas_call(slab_kernel, out_shape=jax.ShapeDtypeStruct((2, 8, 8, cell...]
where the time goes in v2:
time: 24.8 us; the launch traced here: 24.5 us
  Pallas kernels  22.3 us (90%)
  other arithmetic  1.53 us (6%)
  between operations  0.64 us (3%)
    pallas_call x1, Pallas kernels, slab_shards(): pl.pallas_call(slab_kernel, out_shape=jax.ShapeDtypeStruct((2, 8, 8, cell...  22.3 us
    div x1, other arithmetic, slab_shards(): var = (second - first * mean) / (QUARTERS - 1)  1.53 us

profile of v2, /device:TPU:0, one launch (start us, length us, event | category | flops | bytes accessed | tf_op | source)
XLA Modules:
  0.0 24.5 jit_solution(17611088245866286180)
XLA Ops:
  0.6 22.3 %shard_map.50 = f32[2,8,8,256]{3,2,1,0:T(8,128)} custom-call(f32[2,64,512]{2,1,0:T(8,128)} %bitcast.2, f32[8,8,256]{2,1,0:T(8,128)} %bitcast.3, bf16[2,2,512,256]{3,2,1,0:T(8,128)(2,1)} %constant.8.clone.table_hbm), custom_call_target="tpu_custom_call" | custom-call | tf_op jit(solution)/shard_map/pallas_call | solution.py:463
  23.0 1.5 %subtract_multiply_fusion = (f32[1,8,8,256]{3,2,1,0:T(8,128)}, f32[1,8,8,256]{3,2,1,0:T(8,128)}) fusion(f32[2,8,8,256]{3,2,1,0:T(8,128)} %shard_map.50), kind=kLoop, calls=%fused_computation | loop fusion | flops 65536 | bytes 262144 | tf_op jit(solution)/shard_map/div | solution.py:483
